TPU v7x, 32 devices: a whole 2x2x4 slice. The times are simulated.
32 devices in a mesh: section: 1, expert: 32 (over z, y, x, core).
Axes of the slice: x: 2, y: 2, z: 4, core: 2. Of those that a mesh axis runs over, the one named last changes fastest.
Arguments:
- hidden: bfloat16 [1, 256, 7168], P('section', 'expert'), may hold values from -6 to 6
- norm_gain: float32 [1, 7168], P('section'), may hold values from 0.25 to 1.75
- w_up: bfloat16 [1, 7168, 4096], P('section', None, 'expert'), may hold values from -0.0625 to 0.0625
- w_down: bfloat16 [1, 4096, 7168], P('section', 'expert'), may hold values from -0.1875 to 0.1875
- expert_ids: int32 [1, 2, 256, 2], P('section', None, 'expert'), may hold values from 0 to 3, all different within a row; in each aligned block of 8 rows (0 to 7, 8 to 15, ..., all dimensions but the last counted through in order) at most 6 rows name the same one
- route_gates: float32 [1, 2, 256, 2], P('section', None, 'expert'), may hold values from 0.25 to 1.5
Outputs:
- advanced: bfloat16 [1, 256, 7168], P('section', 'expert')
Inputs may be any that keep to these rules, and one draw needn't show every extreme that they name: `expert_ids`: the 2 ids of a row differ. In each aligned block of 8 rows (the rows of one device in one pass) no expert is named by more than 6 rows; some expert is named by exactly 6 rows.
All inputs are finite; a program needn't handle non-finite values.
Results may differ from a plain program's by a relative error of at most 0.0085.
Values may be sent and summed in bfloat16 or wider, within the bound.
A program may use at most 64 MiB of HBM per device.

v0:
```python
import jax
import jax.numpy as jnp
from jax import lax
from jax.sharding import PartitionSpec as P

HID = 1024
HID_DEV = 128


def shifted(value, axis, by):
    count = lax.axis_size(axis)
    return lax.ppermute(value, axis, [(i, (i + by) % count) for i in range(count)])


def rms_scale(current, gain_row):
    values = current.astype(jnp.float32)
    inverse_rms = lax.rsqrt(jnp.mean(values * values, axis=-1, keepdims=True) + 1e-06)
    return (values, (values * inverse_rms * gain_row).astype(jnp.bfloat16))


def route_tables(route_ids, gate_values, expert_count, capacity):
    row_count, top_count = route_ids.shape
    flat_ids = route_ids.reshape(-1)
    onehot = (flat_ids[:, None] == jnp.arange(expert_count, dtype=jnp.int32)[None, :]).astype(
        jnp.int32
    )
    earlier = jnp.cumsum(onehot, axis=0) - onehot
    slot_index = jnp.sum(earlier * onehot, axis=1)
    target = flat_ids * capacity + slot_index
    placed = (
        jnp.arange(expert_count * capacity, dtype=jnp.int32)[:, None] == target[None, :]
    ).astype(jnp.float32)
    owners = (
        (jnp.arange(row_count * top_count, dtype=jnp.int32) // top_count)[:, None]
        == jnp.arange(row_count, dtype=jnp.int32)[None, :]
    ).astype(jnp.float32)
    picker = jnp.dot(placed, owners, precision=lax.Precision.HIGHEST)
    weigher = jnp.dot(
        placed * gate_values.reshape(-1)[None, :], owners, precision=lax.Precision.HIGHEST
    )
    return (picker.astype(jnp.bfloat16), weigher)


def expert_apply(received, up_slice, down_slice):
    flat_rows = received.reshape(-1, received.shape[-1])
    upward = jnp.dot(flat_rows, up_slice, preferred_element_type=jnp.float32)
    active = jax.nn.silu(upward).astype(jnp.bfloat16)
    partial_out = jnp.dot(active, down_slice, preferred_element_type=jnp.float32).astype(
        jnp.bfloat16
    )
    return partial_out.reshape(received.shape)


def body(hidden, norm_gain, w_up, w_down, expert_ids, route_gates):
    model_width = hidden.shape[-1]
    group_size = HID // HID_DEV
    devices = lax.axis_size("expert")
    expert_count = devices // group_size
    row_count = hidden.shape[1]
    top_count = expert_ids.shape[-1]
    capacity = min(row_count, (row_count * top_count + expert_count - 1) // expert_count + 2)
    up_slice = w_up[0]
    down_slice = w_down[0]
    gain_row = norm_gain[0]
    current = hidden[0]
    for pass_index in range(expert_ids.shape[1]):
        values, normed = rms_scale(current, gain_row)
        picker, weigher = route_tables(
            expert_ids[0, pass_index], route_gates[0, pass_index], expert_count, capacity
        )
        packed = jnp.dot(picker, normed, preferred_element_type=jnp.float32).astype(jnp.bfloat16)
        copies = jnp.broadcast_to(
            packed.reshape(expert_count, 1, capacity, model_width),
            (expert_count, group_size, capacity, model_width),
        )
        copies = copies.reshape(devices, capacity, model_width)
        partial_out = expert_apply(
            lax.all_to_all(copies, "expert", split_axis=0, concat_axis=0, tiled=True),
            up_slice,
            down_slice,
        )
        returned = lax.all_to_all(partial_out, "expert", split_axis=0, concat_axis=0, tiled=True)
        outputs = jnp.sum(
            returned.reshape(expert_count, group_size, capacity, model_width).astype(jnp.float32),
            axis=1,
        )
        mixture = jnp.dot(
            weigher.T,
            outputs.reshape(expert_count * capacity, model_width),
            precision=lax.Precision.HIGHEST,
            preferred_element_type=jnp.float32,
        )
        updated = (values + mixture).astype(jnp.bfloat16)
        current = shifted(updated, "section", 1)
    return current[None]


def solution(mesh):
    placed = (
        P("section", "expert", None),
        P("section", None),
        P("section", None, "expert"),
        P("section", "expert", None),
        P("section", None, "expert", None),
        P("section", None, "expert", None),
    )
    return jax.shard_map(
        body, mesh=mesh, in_specs=placed, out_specs=P("section", "expert", None), check_vma=False
    )
```

profile of v0, /device:TPU:0, one launch (start us, length us, event | category | flops | bytes accessed | tf_op | source)
XLA Modules:
  0.0 395.4 jit_solution(15515834560095142348)
XLA Ops:
  0.0 0.0 copy-start
  0.0 0.8 fusion.53
  0.8 0.1 copy.11
  0.9 0.1 reshape_squeeze.6
  1.0 0.1 fusion.36
  1.1 0.2 select_reduce_fusion.1
  1.3 0.0 copy-start.4
  1.3 1.1 fusion.11
  2.4 0.2 convolution_convert_fusion.5
  2.6 1.2 convolution_convert_fusion.3
  3.8 0.1 broadcast_in_dim.10
  3.9 0.4 broadcast_in_dim.11
  4.4 90.2 %all_to_all.20 = bf16[32,6,7168]{2,1,0:T(8,128)(2,1)} all-to-all(bf16[32,6,7168]{2,1,0:T(8,128)(2,1)S(1)} %bitcast.52), channel_id=1, replica_groups=mesh['section'=1,'expert'=32] {'expert'}, dimensions={0} | all-to-all | bytes 5505024 | tf_op jit(solution)/shard_map/all_to_all | solution.py:78
  94.5 4.6 %reshape.86 = bf16[192,7168]{1,0:T(8,128)(2,1)} reshape(bf16[32,6,7168]{2,1,0:T(8,128)(2,1)} %all_to_all.20) | data formatting | bytes 5505024 | tf_op jit(solution)/shard_map/reshape | solution.py:45
  99.2 0.0 copy-done
  99.2 5.6 %convolution_convert_fusion.1 = bf16[192,7168]{1,0:T(8,128)(2,1)} fusion(bf16[1,128,7168]{2,1,0:T(8,128)(2,1)S(1)} %copy-done, bf16[192,7168]{1,0:T(8,128)(2,1)} %reshape.86, bf16[1,7168,128]{2,1,0:T(8,128)(2,1)} %param.8), kind=kOutput, calls=%fused_computation.1 | convolution fusion | flops 706142208 | bytes 9175040 | tf_op jit(solution)/shard_map/dot_general | solution.py:48
  104.7 4.6 %reshape.87 = bf16[32,6,7168]{2,1,0:T(8,128)(2,1)} reshape(bf16[192,7168]{1,0:T(8,128)(2,1)} %convolution_convert_fusion.1) | data formatting | bytes 5505024 | tf_op jit(solution)/shard_map/reshape | solution.py:51
  109.3 0.0 copy-start.3
  109.3 3.7 all-to-all-start.1
  113.0 0.0 copy-done.3
  113.0 0.6 fusion.54
  113.6 0.1 copy.12
  113.7 0.1 mul.87
  113.7 0.1 copy.13
  113.8 0.1 reshape_squeeze.7
  113.9 0.1 fusion.35
  114.0 0.2 select_reduce_fusion
  114.2 0.5 multiply_add_fusion
  114.7 0.0 copy-done.4
  114.7 0.8 fusion.33
  115.5 0.0 copy-start.1
  115.5 80.2 %all-to-all-done.1 = bf16[32,6,7168]{2,1,0:T(8,128)(2,1)} async-done(((bf16[32,6,7168]{2,1,0:T(8,128)(2,1)}), bf16[32,6,7168]{2,1,0:T(8,128)(2,1)}, u32[]{:S(2)}, u32[]{:S(2)}) %all-to-all-start.1) | async-done | bytes 2752544 | tf_op jit(solution)/shard_map/all_to_all | solution.py:82
  195.7 2.9 convert_reduce_fusion.1
  198.6 0.1 reshape.88
  198.7 0.0 copy-done.1
  198.7 1.2 fusion
  200.0 0.0 collective-permute-start
  200.0 0.9 convolution_convert_fusion.4
  200.9 0.0 collective-permute-done
  200.9 0.2 fusion.8
  201.1 1.1 convolution_convert_fusion.2
  202.1 0.1 broadcast_in_dim.12
  202.2 0.4 broadcast_in_dim.13
  202.7 86.7 %all_to_all.21 = bf16[32,6,7168]{2,1,0:T(8,128)(2,1)} all-to-all(bf16[32,6,7168]{2,1,0:T(8,128)(2,1)S(1)} %bitcast.53), channel_id=1, replica_groups=mesh['section'=1,'expert'=32] {'expert'}, dimensions={0} | all-to-all | bytes 5505024 | tf_op jit(solution)/shard_map/all_to_all | solution.py:78
  289.4 4.6 %reshape.90 = bf16[192,7168]{1,0:T(8,128)(2,1)} reshape(bf16[32,6,7168]{2,1,0:T(8,128)(2,1)} %all_to_all.21) | data formatting | bytes 5505024 | tf_op jit(solution)/shard_map/reshape | solution.py:45
  294.0 5.6 %convolution_convert_fusion = bf16[192,7168]{1,0:T(8,128)(2,1)} fusion(bf16[1,128,7168]{2,1,0:T(8,128)(2,1)S(1)} %copy-done, bf16[192,7168]{1,0:T(8,128)(2,1)} %reshape.90, bf16[1,7168,128]{2,1,0:T(8,128)(2,1)} %param.8), kind=kOutput, calls=%fused_computation | convolution fusion | flops 706142208 | bytes 9175040 | tf_op jit(solution)/shard_map/dot_general | solution.py:48
  299.6 4.6 %reshape.91 = bf16[32,6,7168]{2,1,0:T(8,128)(2,1)} reshape(bf16[192,7168]{1,0:T(8,128)(2,1)} %convolution_convert_fusion) | data formatting | bytes 5505024 | tf_op jit(solution)/shard_map/reshape | solution.py:51
  304.2 0.0 copy-start.2
  304.2 0.0 copy-start.5
  304.2 0.0 copy-start.6
  304.2 3.6 all-to-all-start.3
  307.7 0.0 copy-done.2
  307.7 0.1 copy.14
  307.8 0.1 mul.99
  307.9 0.0 copy-done.5
  307.9 0.0 copy-done.6
  307.9 0.8 fusion.31
  308.7 81.7 %all-to-all-done.3 = bf16[32,6,7168]{2,1,0:T(8,128)(2,1)} async-done(((bf16[32,6,7168]{2,1,0:T(8,128)(2,1)}), bf16[32,6,7168]{2,1,0:T(8,128)(2,1)}, u32[]{:S(2)}, u32[]{:S(2)}) %all-to-all-start.3) | async-done | bytes 2752544 | tf_op jit(solution)/shard_map/all_to_all | solution.py:82
  390.5 2.9 convert_reduce_fusion
  393.4 0.1 reshape.92
  393.5 1.2 fusion.1
  394.7 0.0 collective-permute-start.1
  394.7 0.0 collective-permute-done.1
  394.7 0.6 copy.16
  (5 shorter events, 0.1 us)
Async XLA Ops:
  0.0 99.2 %copy-start = (bf16[1,128,7168]{2,1,0:T(8,128)(2,1)S(1)}, bf16[1,128,7168]{2,1,0:T(8,128)(2,1)}, u32[]{:S(2)}) copy-start(bf16[1,128,7168]{2,1,0:T(8,128)(2,1)} %param.9) | copy-start | bytes 5505028
  1.3 113.4 %copy-start.4 = (s32[16]{0:T(128)}, s32[16]{0:T(128)S(1)}, u32[]{:S(2)}) copy-start(s32[16]{0:T(128)S(1)} %get-tuple-element.9) | copy-start | bytes 196
  109.3 3.7 copy-start.3
  109.3 86.4 %all-to-all-start.1 = ((bf16[32,6,7168]{2,1,0:T(8,128)(2,1)}), bf16[32,6,7168]{2,1,0:T(8,128)(2,1)}, u32[]{:S(2)}, u32[]{:S(2)}) async-start(bf16[32,6,7168]{2,1,0:T(8,128)(2,1)} %reshape.87), calls=%async_computation.1 | async-start | bytes 7340032 | tf_op jit(solution)/shard_map/all_to_all | solution.py:82
  115.5 83.2 %copy-start.1 = (bf16[1,8,7168]{2,1,0:T(8,128)(2,1)S(1)}, bf16[1,8,7168]{2,1,0:T(8,128)(2,1)}, u32[]{:S(2)}) copy-start(bf16[1,8,7168]{2,1,0:T(8,128)(2,1)} %param.6) | copy-start | bytes 344068
  200.0 0.9 collective-permute-start
  304.2 3.6 copy-start.2
  304.2 3.7 copy-start.5
  304.2 3.7 copy-start.6
  304.2 86.3 %all-to-all-start.3 = ((bf16[32,6,7168]{2,1,0:T(8,128)(2,1)}), bf16[32,6,7168]{2,1,0:T(8,128)(2,1)}, u32[]{:S(2)}, u32[]{:S(2)}) async-start(bf16[32,6,7168]{2,1,0:T(8,128)(2,1)} %reshape.91), calls=%async_computation.3 | async-start | bytes 7340032 | tf_op jit(solution)/shard_map/all_to_all | solution.py:82
  (1 other events, 0.0 us)
where the time goes:
time: 396 us; the launch traced here: 395 us
  blocking collectives  177 us (45%)
  waiting for transfers between devices  162 us (41%)
  local copies, waits for them, and re-layouts  22.5 us (6%)
  matrix products  18.5 us (5%)
  other arithmetic  8.15 us (2%)
  starting transfers between devices  7.25 us (2%)
    all_to_all x2, blocking collectives, body(): lax.all_to_all(copies, 'expert', split_axis=0, concat_axis=0, tiled=True)  177 us
    all_to_all x2, waiting for transfers between devices, body(): lax.all_to_all(partial_out, 'expert', split_axis=0, concat_axis=0, tiled=...  162 us
    dot_general x2, matrix products, expert_apply(): jnp.dot(active, down_slice, preferred_element_type=jnp.float32)  11.1 us
    reshape x2, local copies, waits for them, and re-layouts, expert_apply(): flat_rows = received.reshape(-1, received.shape[-1])  9.27 us
    reshape x2, local copies, waits for them, and re-layouts, expert_apply(): return partial_out.reshape(received.shape)  9.21 us
  transfers between devices with their start and end apart: 4, of which 2 were waited for; matrix products, arithmetic and copies ran while one was open for 1% of the time, Pallas kernels for 0%

commit v1 on v0

v1 whole, which is shorter than its diff:
```python
import functools

import jax
import jax.numpy as jnp
from jax import lax
from jax.experimental import pallas as pl
from jax.experimental.pallas import tpu as pltpu
from jax.sharding import PartitionSpec as P

HID = 1024
HID_DEV = 128
CHUNKS = 4
CHIPS = HID // HID_DEV // 2


def kernel(
    planes, sections, passes,
    hidden, gain, ids, gates, up_hbm, down_hbm, out,
    up, down, rows, meta, part, first, second_out, second, plane_sum, plane_in, cur, shift_out, shift_in,
    w_local, w_send, w_recv, meta_send, meta_recv, zag_send, zag_recv, pag_send, pag_recv,
    one_send, one_recv, two_send, two_recv, zrs_send, zrs_recv, sh_send, sh_recv,
):
    me = lax.axis_index("expert")
    core = lax.rem(me, 2)
    chip = lax.rem(me // 2, CHIPS)
    plane = me // (2 * CHIPS)
    half = cur.shape[2]
    wide = half // CHUNKS
    mate = {1: chip + 1 - 2 * lax.rem(chip, 2), 2: lax.rem(chip + 2, 4), 3: 3 - chip}

    def at(plane_index, chip_index, core_index):
        return {"expert": (plane_index * CHIPS + chip_index) * 2 + core_index}

    def plane_at(by):
        return lax.rem(plane + by + planes, planes)

    partner = at(plane, chip, 1 - core)
    peers = [at(plane_at(d), chip, core) for d in range(1, planes)]
    mates = {k: at(plane, mate[k], core) for k in (1, 2)}
    targets = [partner, mates[1], mates[2]] + peers
    if sections > 1:
        sec = lax.axis_index("section")
        after = {"section": lax.rem(sec + 1, sections)}
        before = {"section": lax.rem(sec + sections - 1, sections)}
        targets = targets + [after, before]
    barrier = pltpu.get_barrier_semaphore()
    for target in targets:
        pl.semaphore_signal(barrier, inc=1, device_id=target, device_id_type=pl.DeviceIdType.MESH)
    pl.semaphore_wait(barrier, len(targets))

    pending = []

    def remote(src, dst, send, recv, target):
        return pltpu.make_async_remote_copy(
            src_ref=src, dst_ref=dst, send_sem=send, recv_sem=recv,
            device_id=target, device_id_type=pl.DeviceIdType.MESH,
        )

    def send(*args):
        copy = remote(*args)
        copy.start()
        pending.append(copy)

    lanes = lax.broadcasted_iota(jnp.int32, (ids.shape[1], 128), 1)
    table = jnp.zeros((ids.shape[1], 128), jnp.float32)
    for p in range(passes):
        for k in range(ids.shape[2]):
            hit = lanes == ids[p, :, k : k + 1] + p * planes
            table = table + jnp.where(hit, gates[p, :, k : k + 1], 0.0)
    meta[chip, plane] = table
    for d in range(1, planes):
        send(meta.at[chip, plane], meta.at[chip, plane], meta_send.at[d - 1], meta_recv.at[d - 1], peers[d - 1])

    for h in range(2):
        cur[h] = hidden[:, h * half : (h + 1) * half].astype(jnp.float32)

    def gather_z(p):
        a, b = cur[0], cur[1]
        total = jnp.sum(a * a, axis=-1, keepdims=True) + jnp.sum(b * b, axis=-1, keepdims=True)
        scale = lax.rsqrt(total / (2 * half) + 1e-06)
        for c in range(CHUNKS):
            lo, hi = c * wide, (c + 1) * wide
            top = cur[0, :, lo:hi] * scale * gain[:, lo:hi]
            bottom = cur[1, :, lo:hi] * scale * gain[:, half + lo : half + hi]
            rows[p, c, chip, plane] = jnp.concatenate([top, bottom], axis=0).astype(jnp.bfloat16)
            block = rows.at[p, c, chip, plane]
            for d in range(1, planes):
                send(block, block, zag_send.at[p, c, d - 1], zag_recv.at[p, c, d - 1], peers[d - 1])

    def order(c):
        return (1, 2) if c % 2 == 0 else (2, 1)

    gather_z(0)
    locals_ = [
        pltpu.make_async_copy(up_hbm, up.at[:, pl.ds(0, HID_DEV)], w_local.at[0]),
        pltpu.make_async_copy(down_hbm, down.at[pl.ds(0, HID_DEV)], w_local.at[1]),
    ]
    for copy in locals_:
        copy.start()
    up_copy = remote(up_hbm, up.at[:, pl.ds(HID_DEV, HID_DEV)], w_send.at[0], w_recv.at[0], partner)
    down_copy = remote(down_hbm, down.at[pl.ds(HID_DEV, HID_DEV)], w_send.at[1], w_recv.at[1], partner)
    up_copy.start()
    down_copy.start()

    for d in range(1, planes):
        src = meta.at[chip, plane_at(-d)]
        remote(src, src, meta_send.at[d - 1], meta_recv.at[d - 1], peers[d - 1]).wait_recv()
    slot = planes - 1
    for i, k in enumerate((1, 2)):
        send(meta.at[chip], meta.at[chip], meta_send.at[slot + i], meta_recv.at[slot + i], mates[k])

    def meta_forward():
        src = meta.at[mate[1]]
        remote(src, src, meta_send.at[slot], meta_recv.at[slot], mates[1]).wait_recv()
        send(src, src, meta_send.at[slot + 2], meta_recv.at[slot + 2], mates[2])

    def meta_finish():
        for i, k in ((1, 2), (2, 3)):
            src = meta.at[mate[k]]
            remote(src, src, meta_send.at[slot + i], meta_recv.at[slot + i], mates[2]).wait_recv()

    for p in range(passes):
        if p > 0:
            gather_z(p)
        top_sum = bottom_sum = None
        for step in range(CHUNKS + 2):
            if step < CHUNKS:
                c = step
                for d in range(1, planes):
                    src = rows.at[p, c, chip, plane_at(-d)]
                    remote(src, src, zag_send.at[p, c, d - 1], zag_recv.at[p, c, d - 1], peers[d - 1]).wait_recv()
                for i, k in enumerate(order(c)):
                    src = rows.at[p, c, chip]
                    send(src, src, pag_send.at[p, c, i], pag_recv.at[p, c, i], mates[k])
            if 1 <= step <= CHUNKS:
                c = step - 1
                near, far = order(c)
                src = rows.at[p, c, mate[near]]
                remote(src, src, pag_send.at[p, c, 0], pag_recv.at[p, c, 0], mates[near]).wait_recv()
                send(src, src, pag_send.at[p, c, 2], pag_recv.at[p, c, 2], mates[far])
                if p == 0 and step == 1:
                    meta_forward()
            if step >= 2:
                c = step - 2
                near, far = order(c)
                for i, k in ((1, far), (2, 3)):
                    src = rows.at[p, c, mate[k]]
                    remote(src, src, pag_send.at[p, c, i], pag_recv.at[p, c, i], mates[far]).wait_recv()
                if p == 0 and c == 0:
                    locals_[0].wait()
                    up_copy.wait_recv()
                block = rows[p, c].reshape(CHIPS * planes * 16, wide)
                top = jnp.dot(block, up[c * wide : (c + 1) * wide, :], preferred_element_type=jnp.float32)
                bottom = jnp.dot(
                    block, up[half + c * wide : half + (c + 1) * wide, :], preferred_element_type=jnp.float32
                )
                top_sum = top if c == 0 else top_sum + top
                bottom_sum = bottom if c == 0 else bottom_sum + bottom
        if p == 0:
            meta_finish()
            locals_[1].wait()
            down_copy.wait_recv()
        upward = (
            top_sum.reshape(CHIPS * planes, 2, 8, 2 * HID_DEV)[:, 0]
            + bottom_sum.reshape(CHIPS * planes, 2, 8, 2 * HID_DEV)[:, 1]
        ).reshape(CHIPS * planes * 8, 2 * HID_DEV)
        tables = meta[...].reshape(CHIPS * planes * 8, 128)
        mine = lax.broadcasted_iota(jnp.int32, tables.shape, 1) == plane + p * planes
        gate = jnp.sum(jnp.where(mine, tables, 0.0), axis=-1, keepdims=True)
        active = (upward / (1.0 + jnp.exp(-upward)) * gate).astype(jnp.bfloat16)
        for c in range(CHUNKS):
            lo, hi = c * wide, (c + 1) * wide
            top = jnp.dot(active, down[:, lo:hi], preferred_element_type=jnp.float32)
            bottom = jnp.dot(active, down[:, half + lo : half + hi], preferred_element_type=jnp.float32)
            both = jnp.concatenate(
                [top.reshape(CHIPS * planes, 8, wide), bottom.reshape(CHIPS * planes, 8, wide)], axis=1
            )
            part[p, c] = both.astype(jnp.bfloat16).reshape(CHIPS, planes, 16, wide)
            near, far = order(c)
            for i, k in ((1, 3), (0, near)):
                send(
                    part.at[p, c, mate[k]], first.at[p, c, i], one_send.at[p, c, i], one_recv.at[p, c, i], mates[near]
                )
        for step in range(CHUNKS + 1):
            if step < CHUNKS:
                c = step
                near, far = order(c)
                src = first.at[p, c, 1]
                remote(src, src, one_send.at[p, c, 1], one_recv.at[p, c, 1], mates[near]).wait_recv()
                total = part[p, c, mate[far]].astype(jnp.float32) + first[p, c, 1].astype(jnp.float32)
                second_out[p, c] = total.astype(jnp.bfloat16)
                send(second_out.at[p, c], second.at[p, c], two_send.at[p, c], two_recv.at[p, c], mates[far])
            if step >= 1:
                c = step - 1
                near, far = order(c)
                src = first.at[p, c, 0]
                remote(src, src, one_send.at[p, c, 0], one_recv.at[p, c, 0], mates[near]).wait_recv()
                src = second.at[p, c]
                remote(src, src, two_send.at[p, c], two_recv.at[p, c], mates[far]).wait_recv()
                total = part[p, c, chip].astype(jnp.float32) + first[p, c, 0].astype(jnp.float32)
                total = total + second[p, c].astype(jnp.float32)
                plane_sum[p, c] = total.astype(jnp.bfloat16)
                for d in range(1, planes):
                    send(
                        plane_sum.at[p, c, plane_at(d)], plane_in.at[p, c, d - 1],
                        zrs_send.at[p, c, d - 1], zrs_recv.at[p, c, d - 1], peers[d - 1],
                    )
        for c in range(CHUNKS):
            lo, hi = c * wide, (c + 1) * wide
            total = plane_sum[p, c, plane].astype(jnp.float32)
            for d in range(1, planes):
                src = plane_in.at[p, c, d - 1]
                remote(src, src, zrs_send.at[p, c, d - 1], zrs_recv.at[p, c, d - 1], peers[d - 1]).wait_recv()
                total = total + plane_in[p, c, d - 1].astype(jnp.float32)
            for h in range(2):
                value = (cur[h, :, lo:hi] + total[h * 8 : h * 8 + 8]).astype(jnp.bfloat16).astype(jnp.float32)
                cur[h, :, lo:hi] = value
        if sections > 1:
            shift_out[p] = jnp.concatenate([cur[0], cur[1]], axis=0).astype(jnp.bfloat16)
            send(shift_out.at[p], shift_in.at[p], sh_send.at[p], sh_recv.at[p], after)
            remote(shift_out.at[p], shift_in.at[p], sh_send.at[p], sh_recv.at[p], after).wait_recv()
            for h in range(2):
                cur[h] = shift_in[p].astype(jnp.float32)[h * 8 : h * 8 + 8]
    for h in range(2):
        out[:, h * half : (h + 1) * half] = cur[h].astype(jnp.bfloat16)
    up_copy.wait_send()
    down_copy.wait_send()
    for copy in pending:
        copy.wait_send()


def body(hidden, norm_gain, w_up, w_down, expert_ids, route_gates):
    width = hidden.shape[-1]
    half = width // 2
    wide = half // CHUNKS
    planes = lax.axis_size("expert") // (2 * CHIPS)
    sections = lax.axis_size("section")
    passes = expert_ids.shape[1]
    bf = jnp.bfloat16
    dma = pltpu.SemaphoreType.DMA
    away = planes - 1
    shift = passes if sections > 1 else 1
    vmem = pl.BlockSpec(memory_space=pltpu.VMEM)
    hbm = pl.BlockSpec(memory_space=pl.ANY)
    result = pl.pallas_call(
        functools.partial(kernel, planes, sections, passes),
        out_shape=jax.ShapeDtypeStruct((8, width), bf),
        in_specs=[vmem] * 4 + [hbm] * 2,
        out_specs=vmem,
        scratch_shapes=[
            pltpu.VMEM((width, 2 * HID_DEV), bf),
            pltpu.VMEM((2 * HID_DEV, width), bf),
            pltpu.VMEM((passes, CHUNKS, CHIPS, planes, 16, wide), bf),
            pltpu.VMEM((CHIPS, planes, 8, 128), jnp.float32),
            pltpu.VMEM((passes, CHUNKS, CHIPS, planes, 16, wide), bf),
            pltpu.VMEM((passes, CHUNKS, 2, planes, 16, wide), bf),
            pltpu.VMEM((passes, CHUNKS, planes, 16, wide), bf),
            pltpu.VMEM((passes, CHUNKS, planes, 16, wide), bf),
            pltpu.VMEM((passes, CHUNKS, planes, 16, wide), bf),
            pltpu.VMEM((passes, CHUNKS, away, 16, wide), bf),
            pltpu.VMEM((2, 8, half), jnp.float32),
            pltpu.VMEM((shift, 16, half), bf),
            pltpu.VMEM((shift, 16, half), bf),
            dma((2,)), dma((2,)), dma((2,)),
            dma((away + 3,)), dma((away + 3,)),
            dma((passes, CHUNKS, away)), dma((passes, CHUNKS, away)),
            dma((passes, CHUNKS, 3)), dma((passes, CHUNKS, 3)),
            dma((passes, CHUNKS, 2)), dma((passes, CHUNKS, 2)),
            dma((passes, CHUNKS)), dma((passes, CHUNKS)),
            dma((passes, CHUNKS, away)), dma((passes, CHUNKS, away)),
            dma((shift,)), dma((shift,)),
        ],
        compiler_params=pltpu.CompilerParams(
            collective_id=0, has_side_effects=True, vmem_limit_bytes=56 * 1024 * 1024
        ),
    )(hidden[0], norm_gain, expert_ids[0], route_gates[0], w_up[0], w_down[0])
    return result[None]


def solution(mesh):
    placed = (
        P("section", "expert", None),
        P("section", None),
        P("section", None, "expert"),
        P("section", "expert", None),
        P("section", None, "expert", None),
        P("section", None, "expert", None),
    )
    return jax.shard_map(
        body, mesh=mesh, in_specs=placed, out_specs=P("section", "expert", None), check_vma=False
    )
```

time: 396 us -> 106 us (0.27)
  blocking collectives: 177 us -> 0 us
  waiting for transfers between devices: 162 us -> 0 us
  Pallas kernels: 0 us -> 101 us
  matrix products: 18.5 us -> 0 us
  local copies, waits for them, and re-layouts: 22.5 us -> 4.27 us
  other arithmetic: 8.15 us -> 0 us
  starting transfers between devices: 7.25 us -> 0 us
    all_to_all x2 -> x0, blocking collectives: 177 us -> none  [body(): lax.all_to_all(copies, 'expert', split_axis=0, concat_axis=0, tiled=True)]
    all_to_all x2 -> x0, waiting for transfers between devices: 162 us -> none  [body(): lax.all_to_all(partial_out, 'expert', split_axis=0, concat_axis=0, tiled=...]
    pallas_call x0 -> x1, Pallas kernels: none -> 101 us  [body(): pl.pallas_call(functools.partial(kernel, planes, sections, passes), out_s...]
    reshape x6 -> x0, local copies, waits for them, and re-layouts: 18.7 us -> none  [the longest x2 9.27 us: expert_apply(): flat_rows = received.reshape(-1, received.shape[-1])]
    dot_general x10 -> x0, matrix products: 18.5 us -> none  [the longest x2 11.1 us: expert_apply(): jnp.dot(active, down_slice, preferred_element_type=jnp.float32)]
    reduce_sum x6 -> x0, other arithmetic: 7.39 us -> none  [the longest x2 5.77 us: body(): jnp.sum(returned.reshape(expert_count, group_size, capacity, model_width)...]
    all_to_all x2 -> x0, starting transfers between devices: 7.23 us -> none  [body(): lax.all_to_all(partial_out, 'expert', split_axis=0, concat_axis=0, tiled=...]
  transfers between devices with their start and end apart: 4 -> 0, of which waited for: 2 -> 0; matrix products, arithmetic and copies ran while one was open for 1% -> 0% of each run, Pallas kernels for 0% -> 0%
where the time goes in v1:
time: 106 us
  Pallas kernels  101 us (95%)
  local copies, waits for them, and re-layouts  4.27 us (4%)
    pallas_call x1, Pallas kernels, body(): pl.pallas_call(functools.partial(kernel, planes, sections, passes), out_s...  101 us

profile of v1, /device:TPU:0, one launch (start us, length us, event | category | flops | bytes accessed | tf_op | source)
XLA Modules:
  0.0 105.7 jit_solution(9934326880244166931)
XLA Ops:
  0.0 1.4 %copy.7.ids = s32[2,8,2]{2,1,0:T(8,128)} copy(s32[2,8,2]{1,2,0:T(2,128)} %bitcast.10) | data formatting | bytes 256 | tf_op jit(solution)/shard_map/squeeze | solution.py:276
  1.4 1.4 %copy.8.gates = f32[2,8,2]{2,1,0:T(8,128)} copy(f32[2,8,2]{1,2,0:T(2,128)} %bitcast.11) | data formatting | bytes 256 | tf_op jit(solution)/shard_map/squeeze | solution.py:276
  2.7 101.4 %shard_map.64 = bf16[8,7168]{1,0:T(8,128)(2,1)} custom-call(bf16[8,7168]{1,0:T(8,128)(2,1)} %bitcast.9, f32[1,7168]{1,0:T(1,128)} %gain.1, s32[2,8,2]{2,1,0:T(8,128)} %copy.7.ids, f32[2,8,2]{2,1,0:T(8,128)} %copy.8.gates, bf16[7168,128]{1,0:T(8,128)(2,1)} %bitcast.6, bf16[128,7168]{1,0:T(8,128)(2,1)} %bitcast.7), custom_call_target="tpu_custom_call" | custom-call | tf_op jit(solution)/shard_map/pallas_call | solution.py:245
  104.1 1.6 %copy.10 = bf16[1,8,7168]{2,1,0:T(8,128)(2,1)} copy(bf16[1,8,7168]{2,1,0:T(8,128)(2,1)} %bitcast.8) | data formatting | bytes 229376
